TPU v7x, 32 devices: a whole 2x2x4 slice. The times are simulated.
32 devices in a mesh: seg: 16 (over z, y, x), tp: 2 (over core).
Axes of the slice: x: 2, y: 2, z: 4, core: 2. Of those that a mesh axis runs over, the one named last changes fastest.
Arguments:
- qkv: bfloat16 [3, 6144, 6144], P(None, 'seg', 'tp'), may hold values from -20 to 20
- note_slot_document: int32 [48], replicated, may hold values from 0 to 7, never falling along the last dimension, each value on 1 to 9 neighbouring positions
- note_rows: int32 [48], replicated, may hold values from 2 to 128, as said below
- out_weight: bfloat16 [6144, 6144], P('seg', 'tp'), may hold values from -0.3125 to 0.3125
Outputs:
- attended: bfloat16 [6144, 6144], P('seg', 'tp')
Inputs may be any that keep to these rules, and one draw needn't show every extreme that they name: `note_slot_document`: slot ids never fall, a document holds 1 to 9 consecutive slots. `note_rows`: live rows of a block come first.
All inputs are finite; a program needn't handle non-finite values.
Results may differ from a plain program's by a relative error of at most 0.014.
Values may be sent and summed in bfloat16 or wider, within the bound.
A program may use at most 128 MiB of HBM per device.

v0:
```python
import jax
import jax.numpy as jnp
from jax import lax
from jax.sharding import PartitionSpec as P

DH = 128
NOTE_BLOCK_ROWS = 128


masked_score = -1e30


def from_behind(x, axis, by):
    length = lax.axis_size(axis)
    pairs = [(i, i + by) for i in range(length) if 0 <= i + by < length]
    return lax.ppermute(x, axis, pairs)


def attend(queries, key_rows, value_rows, query_doc, key_doc):
    scores = jnp.einsum(
        "qhd,khd->hqk", queries, key_rows, preferred_element_type=jnp.float32
    ) * DH ** (-0.5)
    scores = jnp.where((query_doc[:, None] == key_doc[None, :])[None], scores, masked_score)
    row_max = jnp.max(scores, axis=-1, keepdims=True)
    exponent = jnp.exp(scores - row_max)
    weights = (exponent / jnp.sum(exponent, axis=-1, keepdims=True)).astype(jnp.bfloat16)
    mixed = jnp.einsum("hqk,khd->qhd", weights, value_rows, preferred_element_type=jnp.float32)
    return mixed.astype(jnp.bfloat16)


def attend_blocks(queries, key_rows, value_rows, row_docs, key_doc):
    row_count, head_count = (queries.shape[0], queries.shape[1])
    block_rows = min(row_count, 512)
    block_count = row_count // block_rows

    def one_block(query_pair):
        return attend(query_pair[0], key_rows, value_rows, query_pair[1], key_doc)

    mixed = lax.map(
        one_block,
        (
            queries.reshape(block_count, block_rows, head_count, DH),
            row_docs.reshape(block_count, block_rows),
        ),
    )
    return mixed.reshape(row_count, head_count * DH)


def shards(qkv, note_slot_document, note_rows, out_weight):
    row_count = qkv.shape[1]
    head_count = qkv.shape[2] // DH
    slot_count = row_count // NOTE_BLOCK_ROWS
    seg_place = lax.axis_index("seg")
    memory = from_behind(qkv[1:], "seg", 1)
    slot_docs = lax.dynamic_slice_in_dim(note_slot_document, seg_place * slot_count, slot_count)
    slot_live = lax.dynamic_slice_in_dim(note_rows, seg_place * slot_count, slot_count)
    past_first = jnp.maximum(seg_place - 1, 0) * slot_count
    past_docs = jnp.where(
        seg_place > 0, lax.dynamic_slice_in_dim(note_slot_document, past_first, slot_count), -1
    )
    past_live = lax.dynamic_slice_in_dim(note_rows, past_first, slot_count)
    inside_note_block = jnp.arange(row_count) % NOTE_BLOCK_ROWS
    row_docs = jnp.repeat(slot_docs, NOTE_BLOCK_ROWS)
    own_doc = jnp.where(inside_note_block < jnp.repeat(slot_live, NOTE_BLOCK_ROWS), row_docs, -2)
    earlier_document = jnp.where(
        inside_note_block < jnp.repeat(past_live, NOTE_BLOCK_ROWS),
        jnp.repeat(past_docs, NOTE_BLOCK_ROWS),
        -2,
    )
    queries = qkv[0].reshape(row_count, head_count, DH)
    own_keys = qkv[1].reshape(row_count, head_count, DH)
    own_values = qkv[2].reshape(row_count, head_count, DH)
    key_rows = jnp.concatenate([memory[0].reshape(row_count, head_count, DH), own_keys], axis=0)
    value_rows = jnp.concatenate([memory[1].reshape(row_count, head_count, DH), own_values], axis=0)
    mixed_heads = attend_blocks(
        queries, key_rows, value_rows, row_docs, jnp.concatenate([earlier_document, own_doc])
    )
    heads_all = lax.all_gather(mixed_heads, "tp", axis=1, tiled=True)
    summed = jnp.dot(
        heads_all,
        lax.all_gather(out_weight, "seg", axis=0, tiled=True),
        preferred_element_type=jnp.float32,
    )
    return summed.astype(jnp.bfloat16)


def solution(mesh):
    in_specs = (P(None, "seg", "tp"), P(), P(), P("seg", "tp"))
    out_specs = P("seg", "tp")
    return jax.shard_map(shards, mesh=mesh, in_specs=in_specs, out_specs=out_specs, check_vma=False)
```

profile of v0, /device:TPU:17, one launch (start us, length us, event | category | flops | bytes accessed | tf_op | source)
XLA Modules:
  0.0 632.2 jit_solution(1418454776667941152)
XLA Ops:
  6.5 4.8 slice.18
  11.4 6.6 %copy.18 = bf16[2,384,3072]{1,2,0:T(8,128)(2,1)} copy(bf16[2,384,3072]{2,1,0:T(8,128)(2,1)} %slice.18) | data formatting | bytes 9437184
  18.0 3.1 collective-permute-start
  21.1 6.0 fusion.24
  27.1 2.5 copy.19
  29.6 3.0 copy.12
  32.6 4.3 copy.20
  36.9 4.3 copy.9
  41.3 0.1 broadcast_select_fusion
  41.3 0.1 fusion.18
  41.4 0.1 bitcast_select_fusion.4
  41.5 0.1 broadcast_bitcast_fusion
  41.6 0.2 broadcast_compare_fusion
  41.8 82.9 %collective-permute-done = bf16[2,384,3072]{1,2,0:T(8,128)(2,1)} collective-permute-done((bf16[2,384,3072]{1,2,0:T(8,128)(2,1)}, bf16[2,384,3072]{1,2,0:T(8,128)(2,1)}, u32[]{:S(2)}, u32[]{:S(2)}) %collective-permute-start) | collective-permute-done | bytes 4718624 | tf_op jit(solution)/shard_map/ppermute | solution.py:16
  124.7 5.0 fusion.25
  129.7 4.3 copy.11
  134.0 15.6 %fusion.9 = f32[24,768,384]{2,1,0:T(8,128)} fusion(bf16[384,24,128]{0,2,1:T(8,128)(2,1)} %bitcast.35, bf16[384,24,128]{2,0,1:T(8,128)(2,1)S(1)} %copy.12, bf16[384,24,128]{2,0,1:T(8,128)(2,1)} %copy.11), kind=kOutput, calls=%fused_computation.12 | convolution fusion | flops 1821376512 | bytes 35389440 | tf_op jit(solution)/shard_map/while/body/eval_jaxpr/qhd,khd->hqk/dot_general | solution.py:20
  149.6 32.0 %fusion.27 = (f32[24,384]{1,0:T(8,128)S(1)}, f32[24,384,768]{1,2,0:T(8,128)}) fusion(f32[24,768,384]{2,1,0:T(8,128)} %fusion.9, pred[384,768]{0,1:T(8,128)(4,1)S(1)} %broadcast_compare_fusion), kind=kOutput, calls=%fused_computation.38 | output fusion | flops 42468096 | bytes 56954880 | tf_op jit(solution)/shard_map/while/body/eval_jaxpr/sub | solution.py:25
  181.6 13.8 %fusion.13 = bf16[24,128,384]{2,1,0:T(8,128)(2,1)} fusion(f32[24,384,768]{1,2,0:T(8,128)} %get-tuple-element.36, f32[24,384]{1,0:T(8,128)S(1)} %get-tuple-element.35, bf16[384,24,128]{0,2,1:T(8,128)(2,1)S(1)} %bitcast.38, bf16[384,24,128]{0,2,1:T(8,128)(2,1)} %bitcast.40), kind=kOutput, calls=%fused_computation.17 | convolution fusion | flops 1836711936 | bytes 35426304 | tf_op jit(solution)/shard_map/while/body/eval_jaxpr/hqk,khd->qhd/dot_general | solution.py:27
  195.4 0.0 all-gather.5.cloned.1.call-start
  195.5 0.7 all-gather.5.cloned.1.call-update
  196.2 14.7 %all-gather.3.cloned.1.call-done = bf16[384,6144]{0,1:T(8,128)(2,1)} async-done(((bf16[384,3072]{0,1:T(8,128)(2,1)}), bf16[384,6144]{0,1:T(8,128)(2,1)}) %all-gather.3.cloned.1.call-update) | async-done | bytes 4718608 | tf_op jit(solution)/shard_map/all_gather | solution.py:78
  210.9 392.4 %all-gather.5.cloned.1.call-done = bf16[6144,3072]{1,0:T(8,128)(2,1)} async-done(((bf16[384,3072]{1,0:T(8,128)(2,1)}), bf16[6144,3072]{1,0:T(8,128)(2,1)}) %all-gather.5.cloned.1.call-update) | async-done | bytes 37748752 | tf_op jit(solution)/shard_map/all_gather | solution.py:81
  603.4 22.0 %convolution_convert_fusion = bf16[384,3072]{1,0:T(8,128)(2,1)} fusion(bf16[384,6144]{0,1:T(8,128)(2,1)} %all-gather.3.cloned.1.call-done, bf16[6144,3072]{1,0:T(8,128)(2,1)} %all-gather.5.cloned.1.call-done), kind=kOutput, calls=%fused_computation.16 | convolution fusion | flops 14496694272 | bytes 44826624 | tf_op jit(solution)/shard_map/dot_general | solution.py:79
  (9 shorter events, 0.0 us)
Async XLA Ops:
  6.5 204.4 %all-gather.3.cloned.1.call-start = ((), (), s32[]{:S(2)}) async-start(), calls=%async_computation | async-start | bytes 7077888 | tf_op jit(solution)/shard_map/all_gather | solution.py:78
  18.0 106.7 %collective-permute-start = (bf16[2,384,3072]{1,2,0:T(8,128)(2,1)}, bf16[2,384,3072]{1,2,0:T(8,128)(2,1)}, u32[]{:S(2)}, u32[]{:S(2)}) collective-permute-start(bf16[2,384,3072]{1,2,0:T(8,128)(2,1)} %copy.18), channel_id=1, source_target_pairs={{0,2},{2,4},{4,6},{6,8},{8,10},{10,12},{12,14},{14,16},{16,18},{18... | collective-permute-start | bytes 14155784 | tf_op jit(solution)/shard_map/ppermute | solution.py:16
  32.6 8.7 %copy-start.1 = (s32[48]{0:T(128)S(1)}, s32[48]{0:T(128)}, u32[]{:S(2)}) copy-start(s32[48]{0:T(128)} %param.5) | copy-start | bytes 580
  32.6 8.6 %copy-start.2 = (s32[48]{0:T(128)S(1)}, s32[48]{0:T(128)}, u32[]{:S(2)}) copy-start(s32[48]{0:T(128)} %param.6) | copy-start | bytes 580
  149.6 32.0 %copy-start = (bf16[1,384,3072]{1,2,0:T(8,128)(2,1)S(1)}, bf16[1,384,3072]{1,2,0:T(8,128)(2,1)}, u32[]{:S(2)}) copy-start(bf16[1,384,3072]{1,2,0:T(8,128)(2,1)} %copy.9) | copy-start | bytes 7077892
  195.4 407.9 %all-gather.5.cloned.1.call-start = ((), (), s32[]{:S(2)}) async-start(), calls=%async_computation.1 | async-start | bytes 40108032 | tf_op jit(solution)/shard_map/all_gather | solution.py:81
Sparse Core Ops, SparseCore 0:
  195.6 15.3 all-gather.2
  213.7 389.6 all-gather.4
where the time goes:
time: 636 us; the launch traced here: 632 us
  waiting for transfers between devices  491 us (77%)
  matrix products  51.4 us (8%)
  local copies, waits for them, and re-layouts  40.9 us (6%)
  other arithmetic  32.5 us (5%)
  between operations  13.5 us (2%)
    all_gather x1, waiting for transfers between devices, shards(): lax.all_gather(out_weight, 'seg', axis=0, tiled=True)  392 us
    ppermute x1, waiting for transfers between devices, from_behind(): return lax.ppermute(x, axis, pairs)  82.9 us
    sub x1, other arithmetic, attend(): exponent = jnp.exp(scores - row_max)  32 us
    dot_general x1, matrix products, shards(): jnp.dot(heads_all, lax.all_gather(out_weight, 'seg', axis=0, tiled=True),...  22 us
    dot_general x1, matrix products, attend(): jnp.einsum('qhd,khd->hqk', queries, key_rows, preferred_element_type=jnp....  15.6 us
    all_gather x1, waiting for transfers between devices, shards(): heads_all = lax.all_gather(mixed_heads, 'tp', axis=1, tiled=True)  14.7 us
    dot_general x1, matrix products, attend(): jnp.einsum('hqk,khd->qhd', weights, value_rows, preferred_element_type=jn...  13.8 us
    unnamed x9, local copies, waits for them, and re-layouts  13.4 us
  transfers between devices with their start and end apart: 3, of which 3 were waited for; matrix products, arithmetic and copies ran while one was open for 3% of the time, Pallas kernels for 0%

commit v1 on v0

--- a/solution.py
+++ b/solution.py
@@ -1,6 +1,8 @@
 import jax
 import jax.numpy as jnp
 from jax import lax
+from jax.experimental import pallas as pl
+from jax.experimental.pallas import tpu as pltpu
 from jax.sharding import PartitionSpec as P
 
 DH = 128
@@ -84,7 +86,324 @@
     return summed.astype(jnp.bfloat16)
 
 
+PLANE = 4
+LINE = 4
+CHUNKS = 4
+LOG2_E = 1.4426950408889634
+MESH = pl.DeviceIdType.MESH
+
+
+def fused(
+    docs, live, qkv, w, out, x, wv, mixed, bias, give, take, kept, done,
+    x_send, x_recv, halo_send, halo_recv, w_send, w_recv, core_send, core_recv,
+    sum_send, sum_recv, own_sem, out_sem,
+):
+    seg, tp = lax.axis_index("seg"), lax.axis_index("tp")
+    z, k = seg // PLANE, seg % PLANE
+    kx, ky = k % 2, k // 2
+    rows = qkv.shape[1]
+    width = w.shape[1] // CHUNKS
+    group = w.shape[0]
+    heads = group // DH
+    slots = rows // NOTE_BLOCK_ROWS
+    inner = jnp.logical_and(z > 0, z < LINE - 1)
+
+    def mate(m):
+        px = 1 - kx if m in (1, 3) else kx
+        py = 1 - ky if m in (2, 3) else ky
+        return 2 * py + px
+
+    def at(zz, kk, cc=None):
+        return (zz * PLANE + kk, tp if cc is None else cc)
+
+    barrier = pltpu.get_barrier_semaphore()
+    peers = [at(z, mate(m)) for m in (1, 2, 3)]
+    peers += [at((z + d) % LINE, k) for d in (1, 2, 3)] + [at(z, k, 1 - tp)]
+    for peer in peers:
+        pl.semaphore_signal(barrier, inc=1, device_id=peer, device_id_type=MESH)
+    pl.semaphore_wait(barrier, len(peers))
+
+    def x_copy(t, m):
+        return pltpu.make_async_remote_copy(
+            src_ref=qkv.at[:, :, pl.ds(pl.multiple_of((PLANE * t + mate(m)) * group, DH), group)],
+            dst_ref=x.at[t, k + 1],
+            send_sem=x_send.at[t, m],
+            recv_sem=x_recv.at[t, m],
+            device_id=at(z, mate(m)),
+            device_id_type=MESH,
+        )
+
+    def x_own(t):
+        return pltpu.make_async_copy(
+            qkv.at[:, :, pl.ds(pl.multiple_of((PLANE * t + k) * group, DH), group)],
+            x.at[t, k + 1],
+            x_recv.at[t, 0],
+        )
+
+    def halo_copy(t):
+        return pltpu.make_async_remote_copy(
+            src_ref=x.at[t, PLANE, pl.ds(1, 2)],
+            dst_ref=x.at[t, 0, pl.ds(1, 2)],
+            send_sem=halo_send.at[t],
+            recv_sem=halo_recv.at[t],
+            device_id=at(jnp.minimum(z + 1, LINE - 1), k),
+            device_id_type=MESH,
+        )
+
+    def w_block(zz, n):
+        return wv.at[pl.ds(pl.multiple_of(zz * group, DH), group), pl.ds(n * width, width)]
+
+    def w_copy(slot, step, n):
+        return pltpu.make_async_remote_copy(
+            src_ref=w.at[:, pl.ds(n * width, width)],
+            dst_ref=w_block(z, n),
+            send_sem=w_send.at[slot, n],
+            recv_sem=w_recv.at[z, n],
+            device_id=at(z + step, k),
+            device_id_type=MESH,
+        )
+
+    def w_relay(n):
+        far = 6 - 3 * z
+        return pltpu.make_async_remote_copy(
+            src_ref=w_block(far, n),
+            dst_ref=w_block(far, n),
+            send_sem=w_send.at[4, n],
+            recv_sem=w_recv.at[far, n],
+            device_id=at(3 * z - 3, k),
+            device_id_type=MESH,
+        )
+
+    def w_own(n):
+        return pltpu.make_async_copy(
+            w.at[:, pl.ds(n * width, width)], w_block(z, n), own_sem.at[n]
+        )
+
+    def w_arrived(zz, n):
+        pltpu.make_async_copy(w_block(zz, n), w_block(zz, n), w_recv.at[zz, n]).wait()
+
+    w_steps = ((0, 2), (1, -2), (2, 1), (3, -1))
+
+    def reaches(step):
+        return z < LINE - step if step > 0 else z >= -step
+
+    for t in range(2):
+        for m in (3, 1, 2):
+            x_copy(t, m).start()
+        x_own(t).start()
+    for n in range(CHUNKS):
+        for slot, step in w_steps:
+            @pl.when(reaches(step))
+            def _():
+                w_copy(slot, step, n).start()
+        w_own(n).start()
+
+    @pl.when(z == 0)
+    def _():
+        for t in range(2):
+            x[t, 0, 1:3] = jnp.zeros((2, rows, group), x.dtype)
+
+    place = lax.broadcasted_iota(jnp.int32, (NOTE_BLOCK_ROWS, NOTE_BLOCK_ROWS), 1)
+
+    @pl.loop(0, PLANE)
+    def _(j):
+        first = (z * PLANE + j) * slots
+        for a in range(slots):
+            for b in range(2 * slots):
+                key_slot = first + b - slots
+                safe = jnp.maximum(key_slot, 0)
+                same = jnp.logical_and(docs[safe] == docs[first + a], key_slot >= 0)
+                limit = jnp.where(same, live[safe], 0)
+                bias[
+                    j,
+                    a * NOTE_BLOCK_ROWS : (a + 1) * NOTE_BLOCK_ROWS,
+                    b * NOTE_BLOCK_ROWS : (b + 1) * NOTE_BLOCK_ROWS,
+                ] = jnp.where(place < limit, 0.0, masked_score)
+
+    def attend_rows(t, j):
+        for h in range(heads):
+            lanes = slice(h * DH, (h + 1) * DH)
+            q = x[t, j + 1, 0, :, lanes]
+            scores = [
+                lax.dot_general(
+                    q,
+                    x[t, j + i, 1, :, lanes],
+                    (((1,), (1,)), ((), ())),
+                    preferred_element_type=jnp.float32,
+                )
+                * (DH ** (-0.5) * LOG2_E)
+                + bias[j, :, i * rows : (i + 1) * rows]
+                for i in range(2)
+            ]
+            top = jnp.max(jnp.maximum(scores[0], scores[1]), axis=-1, keepdims=True)
+            powers = [jnp.exp2(s - top) for s in scores]
+            total = jnp.sum(powers[0] + powers[1], axis=-1, keepdims=True)
+            value = sum(
+                jnp.dot(
+                    powers[i].astype(jnp.bfloat16),
+                    x[t, j + i, 2, :, lanes],
+                    preferred_element_type=jnp.float32,
+                )
+                for i in range(2)
+            )
+            column = pl.multiple_of((2 * tp + t) * group + h * DH, DH)
+            mixed[j, :, pl.ds(column, DH)] = (value / total).astype(jnp.bfloat16)
+
+    def core_copy(t, j):
+        part = mixed.at[j, :, pl.ds(pl.multiple_of((2 * tp + t) * group, DH), group)]
+        return pltpu.make_async_remote_copy(
+            src_ref=part,
+            dst_ref=part,
+            send_sem=core_send.at[t, j],
+            recv_sem=core_recv.at[t, j],
+            device_id=at(z, k, 1 - tp),
+            device_id_type=MESH,
+        )
+
+    def relay(n):
+        @pl.when(inner)
+        def _():
+            w_arrived(6 - 3 * z, n)
+            w_relay(n).start()
+
+    for t in range(2):
+        x_own(t).wait()
+        for m in (1, 2, 3):
+            x_copy(t, m).wait_recv()
+
+        @pl.when(z < LINE - 1)
+        def _():
+            halo_copy(t).start()
+
+        relay(t)
+
+        @pl.loop(1, PLANE)
+        def _(j):
+            attend_rows(t, j)
+            core_copy(t, j).start()
+
+    relay(2)
+    for t in range(2):
+        @pl.when(z > 0)
+        def _():
+            halo_copy(t).wait_recv()
+
+        attend_rows(t, 0)
+        core_copy(t, 0).start()
+
+    for t in range(2):
+        for j in range(PLANE):
+            core_copy(t, j).wait_recv()
+
+    def sum_copy(m, n):
+        return pltpu.make_async_remote_copy(
+            src_ref=give.at[m - 1, n],
+            dst_ref=take.at[m - 1, n],
+            send_sem=sum_send.at[m - 1, n],
+            recv_sem=sum_recv.at[m - 1, n],
+            device_id=at(z, mate(m)),
+            device_id_type=MESH,
+        )
+
+    for n in range(CHUNKS):
+        w_own(n).wait()
+        for zz in range(LINE):
+            waited = jnp.logical_and(inner, 6 - 3 * z == zz)
+            @pl.when(jnp.logical_and(z != zz, jnp.logical_not(waited)))
+            def _():
+                w_arrived(zz, n)
+        for m in (3, 1, 2, 0):
+            product = jnp.dot(
+                mixed[mate(m)],
+                wv[:, n * width : (n + 1) * width],
+                preferred_element_type=jnp.float32,
+            )
+            if m == 0:
+                kept[n] = product
+            else:
+                give[m - 1, n] = product.astype(jnp.bfloat16)
+                sum_copy(m, n).start()
+        if n == 1:
+            relay(3)
+
+    def out_copy(n):
+        return pltpu.make_async_copy(
+            done.at[n], out.at[:, pl.ds(n * width, width)], out_sem.at[n]
+        )
+
+    for n in range(CHUNKS):
+        for m in (1, 2, 3):
+            sum_copy(m, n).wait_recv()
+        total = kept[n]
+        for m in (1, 2, 3):
+            total = total + take[m - 1, n].astype(jnp.float32)
+        done[n] = total.astype(jnp.bfloat16)
+        out_copy(n).start()
+
+    for t in range(2):
+        for m in (1, 2, 3):
+            x_copy(t, m).wait_send()
+        for j in range(PLANE):
+            core_copy(t, j).wait_send()
+
+        @pl.when(z < LINE - 1)
+        def _():
+            halo_copy(t).wait_send()
+
+    for n in range(CHUNKS):
+        for slot, step in w_steps:
+            @pl.when(reaches(step))
+            def _():
+                w_copy(slot, step, n).wait_send()
+
+        @pl.when(inner)
+        def _():
+            w_relay(n).wait_send()
+
+        for m in (1, 2, 3):
+            sum_copy(m, n).wait_send()
+        out_copy(n).wait()
+
+
+def fused_shards(qkv, note_slot_document, note_rows, out_weight):
+    rows, group = qkv.shape[1], out_weight.shape[0]
+    columns = out_weight.shape[1]
+    width = columns // CHUNKS
+    dma = pltpu.SemaphoreType.DMA
+    anywhere = pl.BlockSpec(memory_space=pl.ANY)
+    scalars = pl.BlockSpec(memory_space=pltpu.SMEM)
+    return pl.pallas_call(
+        fused,
+        out_shape=jax.ShapeDtypeStruct((rows, columns), jnp.bfloat16),
+        in_specs=[scalars, scalars, anywhere, anywhere],
+        out_specs=anywhere,
+        scratch_shapes=[
+            pltpu.VMEM((2, PLANE + 1, 3, rows, group), jnp.bfloat16),
+            pltpu.VMEM((LINE * group, columns), jnp.bfloat16),
+            pltpu.VMEM((PLANE, rows, LINE * group), jnp.bfloat16),
+            pltpu.VMEM((PLANE, rows, 2 * rows), jnp.float32),
+            pltpu.VMEM((3, CHUNKS, rows, width), jnp.bfloat16),
+            pltpu.VMEM((3, CHUNKS, rows, width), jnp.bfloat16),
+            pltpu.VMEM((CHUNKS, rows, width), jnp.float32),
+            pltpu.VMEM((CHUNKS, rows, width), jnp.bfloat16),
+            dma((2, 4)), dma((2, 4)), dma((2,)), dma((2,)),
+            dma((5, CHUNKS)), dma((LINE, CHUNKS)), dma((2, PLANE)), dma((2, PLANE)),
+            dma((3, CHUNKS)), dma((3, CHUNKS)), dma((CHUNKS,)), dma((CHUNKS,)),
+        ],
+        compiler_params=pltpu.CompilerParams(
+            collective_id=0, has_side_effects=True, vmem_limit_bytes=60 * 2**20
+        ),
+        cost_estimate=pl.CostEstimate(
+            flops=2 * PLANE * rows * LINE * group * columns + 16 * rows * rows * DH * PLANE * 2 * group // DH,
+            bytes_accessed=4 * (qkv.size + 3 * out_weight.size),
+            transcendentals=PLANE * rows * 2 * rows * 2 * group // DH,
+        ),
+    )(note_slot_document, note_rows, qkv, out_weight)
+
+
 def solution(mesh):
     in_specs = (P(None, "seg", "tp"), P(), P(), P("seg", "tp"))
     out_specs = P("seg", "tp")
-    return jax.shard_map(shards, mesh=mesh, in_specs=in_specs, out_specs=out_specs, check_vma=False)
+    in_planes = mesh.shape["seg"] == PLANE * LINE and mesh.shape["tp"] == 2
+    body = fused_shards if in_planes else shards
+    return jax.shard_map(body, mesh=mesh, in_specs=in_specs, out_specs=out_specs, check_vma=False)

time: 636 us -> 296 us (0.47)
  waiting for transfers between devices: 491 us -> 0 us
  Pallas kernels: 0 us -> 292 us
  matrix products: 51.4 us -> 0 us
  local copies, waits for them, and re-layouts: 40.9 us -> 3.22 us
  other arithmetic: 32.5 us -> 0 us
  between operations: 13.5 us -> 0.01 us
    all_gather x2 -> x0, waiting for transfers between devices: 407 us -> none  [the longest x1 392 us: shards(): lax.all_gather(out_weight, 'seg', axis=0, tiled=True)]
    pallas_call x0 -> x1, Pallas kernels: none -> 292 us  [fused_shards(): pl.pallas_call(fused, out_shape=jax.ShapeDtypeStruct((rows, columns), jnp...]
    ppermute x1 -> x0, waiting for transfers between devices: 82.9 us -> none  [from_behind(): return lax.ppermute(x, axis, pairs)]
    dot_general x3 -> x0, matrix products: 51.4 us -> none  [the longest x1 22 us: shards(): jnp.dot(heads_all, lax.all_gather(out_weight, 'seg', axis=0, tiled=True),...]
    sub x1 -> x0, other arithmetic: 32 us -> none  [attend(): exponent = jnp.exp(scores - row_max)]
    slice x4 -> x0, local copies, waits for them, and re-layouts: 20.2 us -> none  [the longest x2 10.3 us: shards(): own_values = qkv[2].reshape(row_count, head_count, DH)]
    unnamed x9 -> x1, local copies, waits for them, and re-layouts: 13.4 us -> 3.22 us
    another operation x2 -> x0, local copies, waits for them, and re-layouts: 7.3 us -> none  [the longest x1 4.26 us: shards(): memory[0].reshape(row_count, head_count, DH)]
  transfers between devices with their start and end apart: 3 -> 0, of which waited for: 3 -> 0; matrix products, arithmetic and copies ran while one was open for 3% -> 0% of each run, Pallas kernels for 0% -> 0%
where the time goes in v1:
time: 296 us
  Pallas kernels  292 us (99%)
  local copies, waits for them, and re-layouts  3.22 us (1%)
    pallas_call x1, Pallas kernels, fused_shards(): pl.pallas_call(fused, out_shape=jax.ShapeDtypeStruct((rows, columns), jnp...  292 us

profile of v1, /device:TPU:17, one launch (start us, length us, event | category | flops | bytes accessed | tf_op | source)
XLA Modules:
  0.0 295.5 jit_solution(3024120545644513032)
XLA Ops:
  0.0 292.3 %shard_map.46 = bf16[384,3072]{1,0:T(8,128)(2,1)} custom-call(s32[48]{0:T(128)} %docs.1, s32[48]{0:T(128)} %live.1, bf16[3,384,3072]{2,1,0:T(8,128)(2,1)} %qkv.1, bf16[384,3072]{1,0:T(8,128)(2,1)} %w.1), custom_call_target="tpu_custom_call" | custom-call | flops 21743271936 | bytes 28311552 | tf_op jit(solution)/shard_map/pallas_call | solution.py:375
  292.3 3.2 %copy.6 = bf16[384,3072]{1,0:T(8,128)(2,1)} copy(bf16[384,3072]{1,0:T(8,128)(2,1)} %shard_map.46) | data formatting | bytes 4718592

commit v2 on v1

--- a/solution.py
+++ b/solution.py
@@ -88,15 +88,15 @@
 
 PLANE = 4
 LINE = 4
-CHUNKS = 4
+CHUNKS = 6
 LOG2_E = 1.4426950408889634
 MESH = pl.DeviceIdType.MESH
 
 
 def fused(
-    docs, live, qkv, w, out, x, wv, mixed, bias, give, take, kept, done,
+    docs, live, qkv, w, out, x, wv, mixed, bias, give, take, passed, landed, kept, later, done,
     x_send, x_recv, halo_send, halo_recv, w_send, w_recv, core_send, core_recv,
-    sum_send, sum_recv, own_sem, out_sem,
+    give_send, give_recv, pass_send, pass_recv, own_sem, out_sem,
 ):
     seg, tp = lax.axis_index("seg"), lax.axis_index("tp")
     z, k = seg // PLANE, seg % PLANE
@@ -191,11 +191,16 @@
         for m in (3, 1, 2):
             x_copy(t, m).start()
         x_own(t).start()
-    for n in range(CHUNKS):
+
+    def w_start(n):
         for slot, step in w_steps:
             @pl.when(reaches(step))
             def _():
                 w_copy(slot, step, n).start()
+
+    w_start(0)
+    w_start(1)
+    for n in range(CHUNKS):
         w_own(n).start()
 
     @pl.when(z == 0)
@@ -276,6 +281,7 @@
             halo_copy(t).start()
 
         relay(t)
+        w_start(t + 2)
 
         @pl.loop(1, PLANE)
         def _(j):
@@ -283,6 +289,8 @@
             core_copy(t, j).start()
 
     relay(2)
+    w_start(4)
+    w_start(5)
     for t in range(2):
         @pl.when(z > 0)
         def _():
@@ -295,36 +303,66 @@
         for j in range(PLANE):
             core_copy(t, j).wait_recv()
 
-    def sum_copy(m, n):
-        return pltpu.make_async_remote_copy(
-            src_ref=give.at[m - 1, n],
-            dst_ref=take.at[m - 1, n],
-            send_sem=sum_send.at[m - 1, n],
-            recv_sem=sum_recv.at[m - 1, n],
-            device_id=at(z, mate(m)),
-            device_id_type=MESH,
-        )
-
-    for n in range(CHUNKS):
+    half = width // 2
+    first = (1, 2)
+
+    def give_copy(n, e):
+        return pltpu.make_async_remote_copy(
+            src_ref=give.at[n, e],
+            dst_ref=take.at[n, e],
+            send_sem=give_send.at[n, e],
+            recv_sem=give_recv.at[n, e],
+            device_id=at(z, mate(first[e])),
+            device_id_type=MESH,
+        )
+
+    def pass_copy(n, e):
+        return pltpu.make_async_remote_copy(
+            src_ref=passed.at[n, e],
+            dst_ref=landed.at[n, e],
+            send_sem=pass_send.at[n, e],
+            recv_sem=pass_recv.at[n, e],
+            device_id=at(z, mate(3 - first[e])),
+            device_id_type=MESH,
+        )
+
+    def multiply(n):
         w_own(n).wait()
         for zz in range(LINE):
             waited = jnp.logical_and(inner, 6 - 3 * z == zz)
             @pl.when(jnp.logical_and(z != zz, jnp.logical_not(waited)))
             def _():
                 w_arrived(zz, n)
-        for m in (3, 1, 2, 0):
-            product = jnp.dot(
+
+        def product(m, e):
+            return jnp.dot(
                 mixed[mate(m)],
-                wv[:, n * width : (n + 1) * width],
+                wv[:, n * width + e * half : n * width + (e + 1) * half],
                 preferred_element_type=jnp.float32,
             )
-            if m == 0:
-                kept[n] = product
-            else:
-                give[m - 1, n] = product.astype(jnp.bfloat16)
-                sum_copy(m, n).start()
-        if n == 1:
-            relay(3)
+
+        for e in range(2):
+            give[n, e, 1] = product(3, e).astype(jnp.bfloat16)
+            give[n, e, 0] = product(first[e], e).astype(jnp.bfloat16)
+            give_copy(n, e).start()
+        for e in range(2):
+            later[n, e] = product(3 - first[e], e)
+            kept[n, e] = product(0, e)
+
+    def pass_on(n):
+        for e in range(2):
+            give_copy(n, e).wait_recv()
+            passed[n, e] = (later[n, e] + take[n, e, 1].astype(jnp.float32)).astype(jnp.bfloat16)
+            pass_copy(n, e).start()
+
+    for n in range(CHUNKS):
+        if n >= 3:
+            relay(n)
+        multiply(n)
+        if n >= 2:
+            pass_on(n - 2)
+    pass_on(CHUNKS - 2)
+    pass_on(CHUNKS - 1)
 
     def out_copy(n):
         return pltpu.make_async_copy(
@@ -332,12 +370,10 @@
         )
 
     for n in range(CHUNKS):
-        for m in (1, 2, 3):
-            sum_copy(m, n).wait_recv()
-        total = kept[n]
-        for m in (1, 2, 3):
-            total = total + take[m - 1, n].astype(jnp.float32)
-        done[n] = total.astype(jnp.bfloat16)
+        for e in range(2):
+            pass_copy(n, e).wait_recv()
+            total = kept[n, e] + take[n, e, 0].astype(jnp.float32) + landed[n, e].astype(jnp.float32)
+            done[n, :, e * half : (e + 1) * half] = total.astype(jnp.bfloat16)
         out_copy(n).start()
 
     for t in range(2):
@@ -360,8 +396,9 @@
         def _():
             w_relay(n).wait_send()
 
-        for m in (1, 2, 3):
-            sum_copy(m, n).wait_send()
+        for e in range(2):
+            give_copy(n, e).wait_send()
+            pass_copy(n, e).wait_send()
         out_copy(n).wait()
 
 
@@ -382,13 +419,17 @@
             pltpu.VMEM((LINE * group, columns), jnp.bfloat16),
             pltpu.VMEM((PLANE, rows, LINE * group), jnp.bfloat16),
             pltpu.VMEM((PLANE, rows, 2 * rows), jnp.float32),
-            pltpu.VMEM((3, CHUNKS, rows, width), jnp.bfloat16),
-            pltpu.VMEM((3, CHUNKS, rows, width), jnp.bfloat16),
-            pltpu.VMEM((CHUNKS, rows, width), jnp.float32),
+            pltpu.VMEM((CHUNKS, 2, 2, rows, width // 2), jnp.bfloat16),
+            pltpu.VMEM((CHUNKS, 2, 2, rows, width // 2), jnp.bfloat16),
+            pltpu.VMEM((CHUNKS, 2, rows, width // 2), jnp.bfloat16),
+            pltpu.VMEM((CHUNKS, 2, rows, width // 2), jnp.bfloat16),
+            pltpu.VMEM((CHUNKS, 2, rows, width // 2), jnp.float32),
+            pltpu.VMEM((CHUNKS, 2, rows, width // 2), jnp.float32),
             pltpu.VMEM((CHUNKS, rows, width), jnp.bfloat16),
             dma((2, 4)), dma((2, 4)), dma((2,)), dma((2,)),
             dma((5, CHUNKS)), dma((LINE, CHUNKS)), dma((2, PLANE)), dma((2, PLANE)),
-            dma((3, CHUNKS)), dma((3, CHUNKS)), dma((CHUNKS,)), dma((CHUNKS,)),
+            dma((CHUNKS, 2)), dma((CHUNKS, 2)), dma((CHUNKS, 2)), dma((CHUNKS, 2)),
+            dma((CHUNKS,)), dma((CHUNKS,)),
         ],
         compiler_params=pltpu.CompilerParams(
             collective_id=0, has_side_effects=True, vmem_limit_bytes=60 * 2**20

time: 296 us -> 225 us (0.76)
  the two profiles are of different devices: /device:TPU:17 before, /device:TPU:26 now
where the time goes in v2:
time: 225 us; the launch traced here: 224 us
  Pallas kernels  221 us (98%)
  local copies, waits for them, and re-layouts  3.22 us (1%)
    pallas_call x1, Pallas kernels, fused_shards(): pl.pallas_call(fused, out_shape=jax.ShapeDtypeStruct((rows, columns), jnp...  221 us

profile of v2, /device:TPU:26, one launch (start us, length us, event | category | flops | bytes accessed | tf_op | source)
XLA Modules:
  0.0 224.5 jit_solution(6313320546392809398)
XLA Ops:
  0.0 221.2 %shard_map.46 = bf16[384,3072]{1,0:T(8,128)(2,1)} custom-call(s32[48]{0:T(128)} %docs.1, s32[48]{0:T(128)} %live.1, bf16[3,384,3072]{2,1,0:T(8,128)(2,1)} %qkv.1, bf16[384,3072]{1,0:T(8,128)(2,1)} %w.1), custom_call_target="tpu_custom_call" | custom-call | flops 21743271936 | bytes 28311552 | tf_op jit(solution)/shard_map/pallas_call | solution.py:412
  221.2 3.2 %copy.6 = bf16[384,3072]{1,0:T(8,128)(2,1)} copy(bf16[384,3072]{1,0:T(8,128)(2,1)} %shard_map.46) | data formatting | bytes 4718592

commit v3 on v2

--- a/solution.py
+++ b/solution.py
@@ -107,6 +107,7 @@
     heads = group // DH
     slots = rows // NOTE_BLOCK_ROWS
     inner = jnp.logical_and(z > 0, z < LINE - 1)
+    pieces = 2 * heads
 
     def mate(m):
         px = 1 - kx if m in (1, 3) else kx
@@ -123,9 +124,13 @@
         pl.semaphore_signal(barrier, inc=1, device_id=peer, device_id_type=MESH)
     pl.semaphore_wait(barrier, len(peers))
 
+    def piece_lanes(t, kk):
+        start = (PLANE * (t // heads) + kk) * group + t % heads * DH
+        return pl.ds(pl.multiple_of(start, DH), DH)
+
     def x_copy(t, m):
         return pltpu.make_async_remote_copy(
-            src_ref=qkv.at[:, :, pl.ds(pl.multiple_of((PLANE * t + mate(m)) * group, DH), group)],
+            src_ref=qkv.at[:, :, piece_lanes(t, mate(m))],
             dst_ref=x.at[t, k + 1],
             send_sem=x_send.at[t, m],
             recv_sem=x_recv.at[t, m],
@@ -135,7 +140,7 @@
 
     def x_own(t):
         return pltpu.make_async_copy(
-            qkv.at[:, :, pl.ds(pl.multiple_of((PLANE * t + k) * group, DH), group)],
+            qkv.at[:, :, piece_lanes(t, k)],
             x.at[t, k + 1],
             x_recv.at[t, 0],
         )
@@ -187,26 +192,37 @@
     def reaches(step):
         return z < LINE - step if step > 0 else z >= -step
 
-    for t in range(2):
+    for t in range(pieces):
         for m in (3, 1, 2):
             x_copy(t, m).start()
         x_own(t).start()
 
-    def w_start(n):
+    def w_start(n, way):
         for slot, step in w_steps:
-            @pl.when(reaches(step))
+            if step * way > 0:
+                go = reaches(step)
+                if abs(step) == 2 and n > 1:
+                    go = jnp.logical_and(go, inner)
+                @pl.when(go)
+                def _():
+                    w_copy(slot, step, n).start()
+
+    for n in range(2):
+        w_start(n, 1)
+        w_start(n, -1)
+    for n in range(2, CHUNKS):
+        for slot, step in w_steps[:2]:
+            @pl.when(jnp.logical_and(reaches(step), jnp.logical_not(inner)))
             def _():
                 w_copy(slot, step, n).start()
-
-    w_start(0)
-    w_start(1)
+    w_start(2, -1)
     for n in range(CHUNKS):
         w_own(n).start()
 
     @pl.when(z == 0)
     def _():
-        for t in range(2):
-            x[t, 0, 1:3] = jnp.zeros((2, rows, group), x.dtype)
+        for t in range(pieces):
+            x[t, 0, 1:3] = jnp.zeros((2, rows, DH), x.dtype)
 
     place = lax.broadcasted_iota(jnp.int32, (NOTE_BLOCK_ROWS, NOTE_BLOCK_ROWS), 1)
 
@@ -226,33 +242,28 @@
                 ] = jnp.where(place < limit, 0.0, masked_score)
 
     def attend_rows(t, j):
-        for h in range(heads):
-            lanes = slice(h * DH, (h + 1) * DH)
-            q = x[t, j + 1, 0, :, lanes]
-            scores = [
-                lax.dot_general(
-                    q,
-                    x[t, j + i, 1, :, lanes],
-                    (((1,), (1,)), ((), ())),
-                    preferred_element_type=jnp.float32,
-                )
-                * (DH ** (-0.5) * LOG2_E)
-                + bias[j, :, i * rows : (i + 1) * rows]
-                for i in range(2)
-            ]
-            top = jnp.max(jnp.maximum(scores[0], scores[1]), axis=-1, keepdims=True)
-            powers = [jnp.exp2(s - top) for s in scores]
-            total = jnp.sum(powers[0] + powers[1], axis=-1, keepdims=True)
-            value = sum(
-                jnp.dot(
-                    powers[i].astype(jnp.bfloat16),
-                    x[t, j + i, 2, :, lanes],
-                    preferred_element_type=jnp.float32,
-                )
-                for i in range(2)
+        scores = [
+            lax.dot_general(
+                x[t, j + 1, 0],
+                x[t, j + i, 1],
+                (((1,), (1,)), ((), ())),
+                preferred_element_type=jnp.float32,
             )
-            column = pl.multiple_of((2 * tp + t) * group + h * DH, DH)
-            mixed[j, :, pl.ds(column, DH)] = (value / total).astype(jnp.bfloat16)
+            * (DH ** (-0.5) * LOG2_E)
+            + bias[j, :, i * rows : (i + 1) * rows]
+            for i in range(2)
+        ]
+        top = jnp.max(jnp.maximum(scores[0], scores[1]), axis=-1, keepdims=True)
+        powers = [jnp.exp2(s - top) for s in scores]
+        total = jnp.sum(powers[0] + powers[1], axis=-1, keepdims=True)
+        value = sum(
+            jnp.dot(
+                powers[i].astype(jnp.bfloat16), x[t, j + i, 2], preferred_element_type=jnp.float32
+            )
+            for i in range(2)
+        )
+        column = pl.multiple_of((2 * tp + t // heads) * group + t % heads * DH, DH)
+        mixed[j, :, pl.ds(column, DH)] = (value / total).astype(jnp.bfloat16)
 
     def core_copy(t, j):
         part = mixed.at[j, :, pl.ds(pl.multiple_of((2 * tp + t) * group, DH), group)]
@@ -271,7 +282,7 @@
             w_arrived(6 - 3 * z, n)
             w_relay(n).start()
 
-    for t in range(2):
+    for t in range(pieces):
         x_own(t).wait()
         for m in (1, 2, 3):
             x_copy(t, m).wait_recv()
@@ -280,24 +291,32 @@
         def _():
             halo_copy(t).start()
 
-        relay(t)
-        w_start(t + 2)
+        if t == pieces // 2 - 1:
+            w_start(2, 1)
+            w_start(3, -1)
+        if t == pieces - 1:
+            for n in range(3, CHUNKS):
+                w_start(n, 1)
+                if n > 3:
+                    w_start(n, -1)
+        if t >= pieces - 4:
+            relay(t - pieces + 4)
 
         @pl.loop(1, PLANE)
         def _(j):
             attend_rows(t, j)
-            core_copy(t, j).start()
-
-    relay(2)
-    w_start(4)
-    w_start(5)
-    for t in range(2):
+            if t % heads == heads - 1:
+                core_copy(t // heads, j).start()
+
+    for t in range(pieces):
         @pl.when(z > 0)
         def _():
             halo_copy(t).wait_recv()
 
         attend_rows(t, 0)
-        core_copy(t, 0).start()
+        if t % heads == heads - 1:
+            core_copy(t // heads, 0).start()
+    relay(4)
 
     for t in range(2):
         for j in range(PLANE):
@@ -356,8 +375,8 @@
             pass_copy(n, e).start()
 
     for n in range(CHUNKS):
-        if n >= 3:
-            relay(n)
+        if n == 1:
+            relay(CHUNKS - 1)
         multiply(n)
         if n >= 2:
             pass_on(n - 2)
@@ -377,10 +396,12 @@
         out_copy(n).start()
 
     for t in range(2):
+        for j in range(PLANE):
+            core_copy(t, j).wait_send()
+
+    for t in range(pieces):
         for m in (1, 2, 3):
             x_copy(t, m).wait_send()
-        for j in range(PLANE):
-            core_copy(t, j).wait_send()
 
         @pl.when(z < LINE - 1)
         def _():
@@ -406,6 +427,7 @@
     rows, group = qkv.shape[1], out_weight.shape[0]
     columns = out_weight.shape[1]
     width = columns // CHUNKS
+    pieces = 2 * group // DH
     dma = pltpu.SemaphoreType.DMA
     anywhere = pl.BlockSpec(memory_space=pl.ANY)
     scalars = pl.BlockSpec(memory_space=pltpu.SMEM)
@@ -415,7 +437,7 @@
         in_specs=[scalars, scalars, anywhere, anywhere],
         out_specs=anywhere,
         scratch_shapes=[
-            pltpu.VMEM((2, PLANE + 1, 3, rows, group), jnp.bfloat16),
+            pltpu.VMEM((pieces, PLANE + 1, 3, rows, DH), jnp.bfloat16),
             pltpu.VMEM((LINE * group, columns), jnp.bfloat16),
             pltpu.VMEM((PLANE, rows, LINE * group), jnp.bfloat16),
             pltpu.VMEM((PLANE, rows, 2 * rows), jnp.float32),
@@ -426,7 +448,7 @@
             pltpu.VMEM((CHUNKS, 2, rows, width // 2), jnp.float32),
             pltpu.VMEM((CHUNKS, 2, rows, width // 2), jnp.float32),
             pltpu.VMEM((CHUNKS, rows, width), jnp.bfloat16),
-            dma((2, 4)), dma((2, 4)), dma((2,)), dma((2,)),
+            dma((pieces, 4)), dma((pieces, 4)), dma((pieces,)), dma((pieces,)),
             dma((5, CHUNKS)), dma((LINE, CHUNKS)), dma((2, PLANE)), dma((2, PLANE)),
             dma((CHUNKS, 2)), dma((CHUNKS, 2)), dma((CHUNKS, 2)), dma((CHUNKS, 2)),
             dma((CHUNKS,)), dma((CHUNKS,)),

time: 225 us -> 220 us (0.978)
  the two profiles are of different devices: /device:TPU:26 before, /device:TPU:17 now
where the time goes in v3:
time: 220 us; the launch traced here: 219 us
  Pallas kernels  216 us (98%)
  local copies, waits for them, and re-layouts  3.22 us (1%)
    pallas_call x1, Pallas kernels, fused_shards(): pl.pallas_call(fused, out_shape=jax.ShapeDtypeStruct((rows, columns), jnp...  216 us

profile of v3, /device:TPU:17, one launch (start us, length us, event | category | flops | bytes accessed | tf_op | source)
XLA Modules:
  0.0 219.0 jit_solution(14209662755550033250)
XLA Ops:
  0.0 215.8 %shard_map.46 = bf16[384,3072]{1,0:T(8,128)(2,1)} custom-call(s32[48]{0:T(128)} %docs.1, s32[48]{0:T(128)} %live.1, bf16[3,384,3072]{2,1,0:T(8,128)(2,1)} %qkv.1, bf16[384,3072]{1,0:T(8,128)(2,1)} %w.1), custom_call_target="tpu_custom_call" | custom-call | flops 21743271936 | bytes 28311552 | tf_op jit(solution)/shard_map/pallas_call | solution.py:434
  215.8 3.2 %copy.6 = bf16[384,3072]{1,0:T(8,128)(2,1)} copy(bf16[384,3072]{1,0:T(8,128)(2,1)} %shard_map.46) | data formatting | bytes 4718592
